TPU v7x, 32 devices: a whole 2x2x4 slice. The times are simulated.
32 devices in a mesh: row: 16 (over z, y, x), col: 2 (over core).
Axes of the slice: x: 2, y: 2, z: 4, core: 2. Of those that a mesh axis runs over, the one named last changes fastest.
Arguments:
- rhs: float32 [2, 16, 1024, 1024], P(None, 'row', None, 'col'), may hold values from -8 to 8
- panels: float32 [2, 2, 16, 1024, 1024], P(None, None, 'row', None, 'col'), may hold values from -0.1875 to 0.1875
- inverses: float32 [2, 1024, 1024], replicated, may hold values from -1 to 4, as said below
Outputs:
- result: float32 [2, 16, 1024, 1024], P(None, 'row', None, 'col')
Inputs may be any that keep to these rules, and one draw needn't show every extreme that they name: Each inverses[k] is lower triangular with a positive diagonal.
All inputs are finite; a program needn't handle non-finite values.
Results may differ from a plain program's by a relative error of at most 0.000075.
Values sent between devices are 32-bit elements; how exact they have to be, the bound alone decides.
A program may use at most 128 MiB of HBM per device.

v0:
```python
import jax
import jax.numpy as jnp
from jax import lax
from jax.sharding import PartitionSpec as P


def broadcast(value, axis, source):
    kept = jnp.where(lax.axis_index(axis) == source, value, 0).astype(value.dtype)
    return lax.psum(kept, axis)


def per_device(rhs, panels, inverses):
    highest = lax.Precision.HIGH
    row_index = lax.axis_index("row")
    row_count = lax.axis_size("row")
    slot_count = rhs.shape[0]
    block_ids = (jnp.arange(slot_count, dtype=jnp.int32) * row_count + row_index)[
        :, None, None, None
    ]

    def solve_block(current, panel_index):
        owner_value = jnp.dot(
            inverses[panel_index], current, precision=highest, preferred_element_type=jnp.float32
        )
        solved = broadcast(owner_value, "row", panel_index)
        return (solved, solved)

    def apply_panel(tiles, solved):
        return jnp.einsum(
            "sqin,nr->sqir",
            lax.all_gather(tiles, "col", axis=3, tiled=True),
            solved,
            precision=highest,
            preferred_element_type=jnp.float32,
        )

    solved0, spread0 = solve_block(rhs[0, 0], 0)
    sectioned = rhs - apply_panel(panels[0], solved0)
    sectioned = jnp.where(block_ids >= 1, sectioned, solved0)
    solved1, spread1 = solve_block(sectioned[0, 0], 1)
    updated = sectioned - apply_panel(panels[1], solved1)
    return jnp.where(block_ids >= 2, updated, jnp.where(block_ids == 1, solved1, sectioned))


def solution(mesh):
    placed = (P(None, "row", None, "col"), P(None, None, "row", None, "col"), P())
    return jax.shard_map(
        per_device,
        mesh=mesh,
        in_specs=placed,
        out_specs=P(None, "row", None, "col"),
        check_vma=False,
    )
```

profile of v0, /device:TPU:24, one launch (start us, length us, event | category | flops | bytes accessed | tf_op | source)
XLA Modules:
  0.0 320.6 jit_solution(399172567072542828)
XLA Ops:
  7.4 0.0 all-reduce.3.cloned.1.call-start
  7.4 7.6 %fusion.20 = f32[1024,512]{1,0:T(8,128)} fusion(f32[2,1,1024,512]{3,2,1,0:T(8,128)} %param.3, f32[2,1024,1024]{2,1,0:T(8,128)} %param.5, pred[]{:T(512)S(6)} %eq.14), kind=kOutput, calls=%fused_computation.20 | convolution fusion | flops 3221749760 | bytes 8388609 | tf_op jit(solution)/shard_map/dot_general | solution.py:22
  15.0 0.0 all-reduce.3.cloned.1.call-update
  15.0 0.0 all-gather.5.cloned.1.call-start
  15.1 7.8 %fusion.27 = (f32[1,2,1,1024,512]{4,3,1,2,0:T(8,128)}, f32[1,2,1,1024,512]{4,3,1,2,0:T(8,128)}) fusion(f32[2,2,1,1024,512]{4,3,1,2,0:T(8,128)} %bitcast.52), kind=kLoop, calls=%fused_computation.25 | loop fusion | bytes 16777216 | tf_op jit(solution)/shard_map/slice | solution.py:41
  22.9 0.0 all-gather.5.cloned.1.call-update
  22.9 0.0 all-gather.7.cloned.1.call-start
  23.0 0.5 all-gather.7.cloned.1.call-update
  23.5 0.2 all-reduce.5.cloned.1.call-start
  23.7 5.4 %copy.6 = f32[2,1,1024,512]{2,3,0,1:T(8,128)} copy(f32[2,1,1024,512]{3,2,1,0:T(8,128)} %param.3) | data formatting | bytes 8388608 | tf_op args[0]
  29.1 111.5 %all-reduce.3.cloned.1.call-done = f32[1024,512]{1,0:T(8,128)} async-done(((f32[1024,512]{1,0:T(8,128)}), f32[1024,512]{1,0:T(8,128)}) %all-reduce.3.cloned.1.call-update) | async-done | bytes 2097168 | tf_op jit(solution)/shard_map/psum | solution.py:9
  140.6 1.9 copy.7
  142.5 0.0 all-gather.5.cloned.1.call-done
  142.6 17.3 %fusion.5 = f32[2,1,1024,512]{2,3,0,1:T(8,128)S(1)} fusion(f32[2,1,1024,512]{2,3,0,1:T(8,128)} %copy.6, f32[1,2,1,1024,1024]{4,3,1,2,0:T(8,128)} %all-gather.5.cloned.1.call-done, f32[1024,512]{1,0:T(8,128)} %all-reduce.3.cloned.1.call-done, f32[1024,512]{0,1:T(8,128)S(1)} %copy.7, pred[2]{0:T(512)(128)(4,1)S(1)} %broadcast_compare_fusion.1), kind=kOutput, calls=%fused_computation.7 | convolution fusion | flops 6444548096 | bytes 20971522 | tf_op jit(solution)/shard_map/sqin,nr->sqir/dot_general | solution.py:29
  159.8 0.0 copy-start
  159.9 2.0 copy-done
  161.9 7.0 %select_bitcast_fusion = f32[1024,512]{0,1:T(8,128)} fusion(f32[2,1024,1024]{2,1,0:T(8,128)} %param.5, f32[2,1,1024,512]{2,3,0,1:T(8,128)S(1)} %fusion.5, pred[]{:T(512)S(6)} %eq.15), kind=kOutput, calls=%fused_computation.18 | convolution fusion | flops 3221749760 | bytes 8388609 | tf_op jit(solution)/shard_map/dot_general | solution.py:22
  168.8 0.0 all-reduce.5.cloned.1.call-update
  168.9 0.0 all-gather.7.cloned.1.call-done
  168.9 125.4 %all-reduce.5.cloned.1.call-done = f32[1024,512]{0,1:T(8,128)} async-done(((f32[1024,512]{0,1:T(8,128)}), f32[1024,512]{0,1:T(8,128)}) %all-reduce.5.cloned.1.call-update) | async-done | bytes 2097168 | tf_op jit(solution)/shard_map/psum | solution.py:9
  294.3 13.4 %fusion.4 = f32[2,1,1024,512]{2,3,0,1:T(8,128)} fusion(f32[2,1,1024,512]{2,3,0,1:T(8,128)} %copy-done, f32[1,2,1,1024,1024]{4,3,1,2,0:T(8,128)} %all-gather.7.cloned.1.call-done, f32[1024,512]{0,1:T(8,128)} %all-reduce.5.cloned.1.call-done, pred[2]{0:T(512)(128)(4,1)S(1)} %get-tuple-element.7, pred[2]{0:T(512)(128)(4,1)S(1)} %get-tuple-element.8), kind=kOutput, calls=%fused_computation.5 | convolution fusion | flops 6445596672 | bytes 18874372 | tf_op jit(solution)/shard_map/sqin,nr->sqir/dot_general | solution.py:29
  307.8 5.4 %copy.9 = f32[2,1,1024,512]{3,2,1,0:T(8,128)} copy(f32[2,1,1024,512]{2,3,0,1:T(8,128)} %fusion.4) | data formatting | bytes 8388608 | tf_op jit(solution)/shard_map/jit(_where)/select_n | solution.py:42
  (2 shorter events, 0.0 us)
Async XLA Ops:
  7.4 133.2 %all-reduce.3.cloned.1.call-start = ((), (), s32[]{:S(2)}) async-start(), calls=%async_computation | async-start | bytes 4194304 | tf_op jit(solution)/shard_map/psum | solution.py:9
  15.0 127.5 %all-gather.5.cloned.1.call-start = ((), (), s32[]{:S(2)}) async-start(), calls=%async_computation.2 | async-start | bytes 12582912 | tf_op jit(solution)/shard_map/all_gather | solution.py:31
  22.9 146.0 %all-gather.7.cloned.1.call-start = ((), (), s32[]{:S(2)}) async-start(), calls=%async_computation.3 | async-start | bytes 12582912 | tf_op jit(solution)/shard_map/all_gather | solution.py:31
  23.5 270.8 %all-reduce.5.cloned.1.call-start = ((), (), s32[]{:S(2)}) async-start(), calls=%async_computation.1 | async-start | bytes 4194304 | tf_op jit(solution)/shard_map/psum | solution.py:9
  159.8 2.0 copy-start
Sparse Core Ops, SparseCore 0:
  15.2 125.3 all-reduce.2
  169.0 125.3 all-reduce.4
Sparse Core Ops, SparseCore 1:
  23.0 21.0 all-gather.4
  45.5 20.9 all-gather.6
where the time goes:
time: 324 us; the launch traced here: 321 us
  waiting for transfers between devices  238 us (73%)
  matrix products  45.3 us (14%)
  local copies, waits for them, and re-layouts  22.5 us (7%)
  between operations  14.9 us (5%)
    psum x2, waiting for transfers between devices, broadcast(): return lax.psum(kept, axis)  237 us
    dot_general x2, matrix products, apply_panel(): jnp.einsum('sqin,nr->sqir', lax.all_gather(tiles, 'col', axis=3, tiled=Tr...  30.7 us
    dot_general x2, matrix products, solve_block(): jnp.dot(inverses[panel_index], current, precision=highest, preferred_elem...  14.6 us
    slice x1, local copies, waits for them, and re-layouts, per_device(): updated = sectioned - apply_panel(panels[1], solved1)  7.8 us
    unnamed x3, local copies, waits for them, and re-layouts  7.38 us
  transfers between devices with their start and end apart: 4, of which 2 were waited for; matrix products, arithmetic and copies ran while one was open for 12% of the time, Pallas kernels for 0%

commit v1 on v0

v1 whole, which is shorter than its diff:
```python
import functools
import random

import jax
import jax.numpy as jnp
from jax import lax
from jax.experimental import pallas as pl
from jax.experimental.pallas import tpu as pltpu
from jax.sharding import PartitionSpec as P

MESH = pl.DeviceIdType.MESH
TREES = 3
CHUNK = 32


def grid_of(n):
    return {16: (4, 2, 2), 64: (4, 4, 4)}.get(n, (n, 1, 1))


def neighbours(n):
    dims = grid_of(n)
    place = lambda z, y, x: (z * dims[1] + y) * dims[2] + x
    table = []
    for axis in range(3):
        for way in (1, -1):
            line = []
            for q in range(n):
                at = [q // (dims[1] * dims[2]), q // dims[2] % dims[1], q % dims[2]]
                at[axis] += way
                line.append(place(*at) if 0 <= at[axis] < dims[axis] else -1)
            table.append(line)
    return table


@functools.lru_cache(maxsize=None)
def spanning_trees(n, root):
    table = neighbours(n)
    edges = [(u, line[u]) for line in table for u in range(n) if line[u] >= 0]
    into = {v: [e for e in edges if e[1] == v] for v in range(n)}
    draw = random.Random(7)
    best = None
    for _ in range(400 if n <= 16 else 25):
        used = {e: 0 for e in edges}
        depth = [{root: 0} for _ in range(TREES)]
        parent = [{} for _ in range(TREES)]
        while any(len(d) < n for d in depth):
            t = min(range(TREES), key=lambda i: (len(depth[i]), draw.random()))
            options = [e for e in edges if e[0] in depth[t] and e[1] not in depth[t]]
            rank = lambda e: (
                used[e],
                depth[t][e[0]] > 0 and e[0] == root,
                depth[t][e[0]],
                sum(used[o] == 0 for o in into[e[1]]),
                draw.random(),
            )
            u, v = min(options, key=rank)
            used[u, v] += 1
            depth[t][v] = depth[t][u] + 1
            parent[t][v] = u
        score = (max(used.values()), sum(c > 1 for c in used.values()), max(max(d.values()) for d in depth))
        if best is None or score < best[0]:
            best = (score, depth, parent)
    _, depth, parent = best
    levels = [[depth[t][q] for q in range(n)] for t in range(TREES)]
    parents = [[parent[t].get(q, (q + 1) % n) for q in range(n)] for t in range(TREES)]
    children = []
    for t in range(TREES):
        lists = [[v for v in range(n) if v != root and parent[t][v] == q] for q in range(n)]
        most = max(len(c) for c in lists)
        children.append([[c[i] if i < len(c) else -1 for c in lists] for i in range(most)])
    return levels, parents, children


def lookup(me, values):
    out = jnp.int32(values[0])
    for q, value in enumerate(values):
        if q and value != values[0]:
            out = jnp.where(me == q, jnp.int32(value), out)
    return out


def spread_kernel(n, root, exchange, *refs):
    if exchange:
        source, panels, out, full, send_sem, recv_sem, own_sem, pan_send, pan_recv, pan_own = refs
    else:
        source, out, send_sem, recv_sem, own_sem = refs
    me = lax.axis_index("row")
    levels, parents, children = spanning_trees(n, root)
    rows = out.shape[0]
    total = rows // CHUNK
    counts = [len(range(t, total, TREES)) for t in range(TREES)]

    level = [lookup(me, v) for v in levels]
    parent = [lookup(me, v) for v in parents]
    child = [[lookup(me, v) for v in lists] for lists in children]
    near = [lookup(me, v) for v in neighbours(n)]

    barrier = pltpu.get_barrier_semaphore()
    for other in near:

        @pl.when(other >= 0)
        def _():
            pl.semaphore_signal(barrier, inc=1, device_id={"row": other}, device_id_type=MESH)

    if exchange:
        core = lax.axis_index("col")
        pl.semaphore_signal(barrier, inc=1, device_id={"col": 1 - core}, device_id_type=MESH)
    peers = [sum(line[q] >= 0 for line in neighbours(n)) for q in range(n)]
    pl.semaphore_wait(barrier, lookup(me, peers) + (1 if exchange else 0))

    @pl.when(me == root)
    def _():
        own = pltpu.make_async_copy(source, out, own_sem)
        own.start()
        own.wait()

    def copy_to(t, j, device, slot):
        part = pl.ds(pl.multiple_of((TREES * j + t) * CHUNK, CHUNK), CHUNK)
        return pltpu.make_async_remote_copy(
            src_ref=out.at[part],
            dst_ref=out.at[part],
            send_sem=send_sem.at[slot, j],
            recv_sem=recv_sem.at[t, j],
            device_id={"row": device},
            device_id_type=MESH,
        )

    slots = []
    for t in range(TREES):
        first = sum(len(c) for c in children[:t])
        slots.append([first + i for i in range(len(children[t]))])

    def panel_copies():
        width = panels.shape[-1]
        columns = pl.ds(pl.multiple_of(core * width, width), width)
        pairs = []
        for k in range(panels.shape[0]):
            target = full.at[k, :, :, columns]
            pairs.append(
                (
                    pltpu.make_async_remote_copy(
                        src_ref=panels.at[k],
                        dst_ref=target,
                        send_sem=pan_send.at[k],
                        recv_sem=pan_recv.at[k],
                        device_id={"col": 1 - core},
                        device_id_type=MESH,
                    ),
                    pltpu.make_async_copy(panels.at[k], target, pan_own.at[k]),
                )
            )
        return pairs

    if exchange:
        for away, home in panel_copies():
            away.start()
            home.start()

    def step(s, carry):
        for t in range(TREES):
            j = s - level[t]

            @pl.when((j >= 0) & (j < counts[t]))
            def _():
                @pl.when(me != root)
                def _():
                    copy_to(t, j, parent[t], slots[t][0]).wait_recv()

                for i, slot in enumerate(slots[t]):

                    @pl.when(child[t][i] >= 0)
                    def _():
                        copy_to(t, j, child[t][i], slot).start()

        return carry

    deepest = max(max(v) for v in levels)
    lax.fori_loop(0, max(counts) + deepest, step, 0)

    for t in range(TREES):

        def finish(j, carry):
            for i, slot in enumerate(slots[t]):

                @pl.when(child[t][i] >= 0)
                def _():
                    copy_to(t, j, child[t][i], slot).wait_send()

            return carry

        lax.fori_loop(0, counts[t], finish, 0)

    if exchange:
        for away, home in panel_copies():
            away.wait()
            home.wait()


def spread(value, n, root, panels=None):
    exchange = panels is not None
    _, _, children = spanning_trees(n, root)
    chunks = -(-(value.shape[0] // CHUNK) // TREES)
    kept = jax.ShapeDtypeStruct(value.shape, value.dtype)
    vmem, anywhere = pl.BlockSpec(memory_space=pltpu.VMEM), pl.BlockSpec(memory_space=pl.ANY)
    scratch = [
        pltpu.SemaphoreType.DMA((sum(len(c) for c in children), chunks)),
        pltpu.SemaphoreType.DMA((TREES, chunks)),
        pltpu.SemaphoreType.DMA,
    ]
    in_specs, out_specs, out_shape, operands = [anywhere], vmem, kept, [value]
    if exchange:
        blocks, slots, rows, width = panels.shape
        in_specs, out_specs, operands = [anywhere] * 2, [vmem, anywhere], [value, panels]
        out_shape = [kept, jax.ShapeDtypeStruct((blocks, slots, rows, 2 * width), panels.dtype)]
        scratch += [pltpu.SemaphoreType.DMA((blocks,))] * 3
    return pl.pallas_call(
        functools.partial(spread_kernel, n, root, exchange),
        out_shape=out_shape,
        in_specs=in_specs,
        out_specs=out_specs,
        scratch_shapes=scratch,
        compiler_params=pltpu.CompilerParams(
            collective_id=1 + root, has_side_effects=True, vmem_limit_bytes=16 * 2**20
        ),
    )(*operands)


def per_device(rhs, panels, inverses):
    n = lax.axis_size("row")
    me = lax.axis_index("row")
    dot = functools.partial(
        jnp.dot, precision=lax.Precision.HIGH, preferred_element_type=jnp.float32
    )
    slots, _, rows, width = rhs.shape
    ids = (jnp.arange(slots, dtype=jnp.int32) * n + me)[:, None, None]
    own = rhs[:, 0]

    first, full = spread(own[0], n, 0, panels[:, :, 0])
    solved0 = dot(inverses[0], first)
    tall = full.reshape(2, slots * rows, full.shape[-1])
    sectioned = own - dot(tall[0], solved0).reshape(slots, rows, width)
    sectioned = jnp.where(ids >= 1, sectioned, solved0)
    solved1 = spread(dot(inverses[1], sectioned[0]), n, 1)
    updated = sectioned - dot(tall[1], solved1).reshape(slots, rows, width)
    result = jnp.where(ids >= 2, updated, jnp.where(ids == 1, solved1, sectioned))
    return result[:, None]


def solution(mesh):
    placed = (P(None, "row", None, "col"), P(None, None, "row", None, "col"), P())
    return jax.shard_map(
        per_device,
        mesh=mesh,
        in_specs=placed,
        out_specs=P(None, "row", None, "col"),
        check_vma=False,
    )
```

time: 324 us -> 139 us (0.43); the launches traced: 321 us -> 139 us
  waiting for transfers between devices: 238 us -> 0 us
  Pallas kernels: 0 us -> 94.7 us
  between operations: 14.9 us -> 0.12 us
  matrix products: 45.3 us -> 31.3 us
  local copies, waits for them, and re-layouts: 22.5 us -> 12.7 us
    psum x2 -> x0, waiting for transfers between devices: 237 us -> none  [broadcast(): return lax.psum(kept, axis)]
    pallas_call x0 -> x2, Pallas kernels: none -> 94.7 us  [spread(): pl.pallas_call(functools.partial(spread_kernel, n, root, exchange), out_s...]
    dot_general x4, matrix products: 45.3 us -> 31.3 us  [the longest x1 10.4 us: per_device(): sectioned = own - dot(tall[0], solved0).reshape(slots, rows, width)]
    slice x1 -> x0, local copies, waits for them, and re-layouts: 7.8 us -> none  [per_device(): updated = sectioned - apply_panel(panels[1], solved1)]
    select_n x1 -> x0, local copies, waits for them, and re-layouts: 5.36 us -> none  [per_device(): jnp.where(block_ids >= 2, updated, jnp.where(block_ids == 1, solved1, sec...]
    unnamed x3 -> x14, local copies, waits for them, and re-layouts: 7.38 us -> 9.13 us
  transfers between devices with their start and end apart: 4 -> 0, of which waited for: 2 -> 0; matrix products, arithmetic and copies ran while one was open for 12% -> 0% of each run, Pallas kernels for 0% -> 0%
where the time goes in v1:
time: 139 us
  Pallas kernels  94.7 us (68%)
  matrix products  31.3 us (23%)
  local copies, waits for them, and re-layouts  12.7 us (9%)
    pallas_call x2, Pallas kernels, spread(): pl.pallas_call(functools.partial(spread_kernel, n, root, exchange), out_s...  94.7 us
    dot_general x1, matrix products, per_device(): sectioned = own - dot(tall[0], solved0).reshape(slots, rows, width)  10.4 us
    unnamed x14, local copies, waits for them, and re-layouts  9.13 us
    dot_general x1, matrix products, per_device(): updated = sectioned - dot(tall[1], solved1).reshape(slots, rows, width)  8.45 us
    dot_general x1, matrix products, per_device(): solved0 = dot(inverses[0], first)  6.86 us
    dot_general x1, matrix products, per_device(): solved1 = spread(dot(inverses[1], sectioned[0]), n, 1)  5.62 us

profile of v1, /device:TPU:24, one launch (start us, length us, event | category | flops | bytes accessed | tf_op | source)
XLA Modules:
  0.0 138.8 jit_solution(9089831335773230177)
XLA Ops:
  0.0 1.8 %slice_bitcast_fusion.2.refs_0_ = f32[1024,512]{1,0:T(8,128)S(1)} fusion(f32[2,1,1024,512]{3,2,1,0:T(8,128)} %param.3), kind=kLoop, calls=%fused_computation.18 | loop fusion | bytes 4194304 | tf_op jit(solution)/shard_map/squeeze | solution.py:238
  1.8 0.0 copy-start.1
  1.8 3.4 %copy-done.1 = f32[2,2,1,1024,512]{4,3,2,1,0:T(8,128)S(1)} copy-done((f32[2,2,1,1024,512]{4,3,2,1,0:T(8,128)S(1)}, f32[2,2,1,1024,512]{4,3,2,1,0:T(8,128)}, u32[]{:S(2)}) %copy-start.1) | copy-done | bytes 8388632
  5.2 0.0 copy-start.2
  5.2 49.4 %shard_map.37 = (f32[1024,512]{1,0:T(8,128)S(1)}, f32[2,2,1024,1024]{3,2,1,0:T(8,128)S(1)}) custom-call(f32[1024,512]{1,0:T(8,128)S(1)} %slice_bitcast_fusion.2.refs_0_, f32[2,2,1024,512]{3,2,1,0:T(8,128)S(1)} %bitcast.50), custom_call_target="tpu_custom_call" | custom-call | tf_op jit(solution)/shard_map/pallas_call | solution.py:216
  54.6 0.0 copy-start
  54.6 5.7 %copy-done = f32[2,2,1024,1024]{3,2,1,0:T(8,128)} copy-done((f32[2,2,1024,1024]{3,2,1,0:T(8,128)}, f32[2,2,1024,1024]{3,2,1,0:T(8,128)S(1)}, u32[]{:S(2)}) %copy-start) | copy-done | bytes 16777240
  60.3 0.0 copy-done.2
  60.3 6.9 %fusion.8 = f32[512,1024]{1,0:T(8,128)S(1)} fusion(f32[1024,512]{1,0:T(8,128)S(1)} %get-tuple-element.8, f32[2,1024,1024]{2,1,0:T(8,128)S(1)} %copy-done.2), kind=kOutput, calls=%fused_computation.8 | convolution fusion | flops 3221225472 | bytes 8388608 | tf_op jit(solution)/shard_map/dot_general | solution.py:239
  67.2 1.8 %copy.4 = f32[1024,512]{1,0:T(8,128)} copy(f32[1024,512]{0,1:T(8,128)S(1)} %bitcast.51) | data formatting | bytes 4194304 | tf_op jit(solution)/shard_map/dot_general | solution.py:239
  69.0 0.0 slice-start
  69.0 0.0 slice-start.1
  69.0 0.0 slice-start.2
  69.0 10.4 %fusion.10 = f32[2,1024,512]{2,1,0:T(8,128)S(1)} fusion(f32[2,1,1024,512]{3,2,1,0:T(8,128)} %param.3, f32[1024,512]{1,0:T(8,128)} %copy.4, pred[2]{0:T(512)(128)(4,1)S(1)} %get-tuple-element.10, f32[512,1024]{1,0:T(8,128)S(1)} %fusion.8, f32[2,2,1024,1024]{3,2,1,0:T(8,128)} %copy-done), kind=kOutput, calls=%fused_computation.11 | convolution fusion | flops 6444548096 | bytes 20971522 | tf_op jit(solution)/shard_map/dot_general | solution.py:241
  79.4 0.0 slice-start.3
  79.4 5.6 %fusion.19.refs_0_ = f32[1024,512]{1,0:T(8,128)S(1)} fusion(f32[2,1024,1024]{2,1,0:T(8,128)} %param.5, f32[2,1024,512]{2,1,0:T(8,128)S(1)} %fusion.10), kind=kOutput, calls=%fused_computation.19 | convolution fusion | flops 3221225472 | bytes 8388608 | tf_op jit(solution)/shard_map/dot_general | solution.py:243
  85.0 45.3 %shard_map.38 = f32[1024,512]{1,0:T(8,128)S(1)} custom-call(f32[1024,512]{1,0:T(8,128)S(1)} %fusion.19.refs_0_), custom_call_target="tpu_custom_call" | custom-call | tf_op jit(solution)/shard_map/pallas_call | solution.py:216
  130.3 0.0 slice-done
  130.3 0.0 slice-done.1
  130.3 0.0 slice-done.2
  130.3 0.0 slice-done.3
  130.4 8.5 %select_bitcast_fusion = f32[2,1,1024,512]{3,2,1,0:T(8,128)} fusion(f32[2,1024,512]{2,1,0:T(8,128)S(1)} %fusion.10, f32[1024,512]{1,0:T(8,128)S(1)} %shard_map.38, pred[2]{0:T(512)(128)(4,1)S(1)} %get-tuple-element.9, pred[2]{0:T(512)(128)(4,1)S(1)} %broadcast_compare_fusion.2, f32[2,2,1024,1024]{3,2,1,0:T(8,128)S(1)} %bitcast.49), kind=kOutput, calls=%fused_computation.12 | convolution fusion | flops 6445596672 | bytes 20972544 | tf_op jit(solution)/shard_map/dot_general | solution.py:244
  (3 shorter events, 0.0 us)
Async XLA Ops:
  1.8 3.4 %copy-start.1 = (f32[2,2,1,1024,512]{4,3,2,1,0:T(8,128)S(1)}, f32[2,2,1,1024,512]{4,3,2,1,0:T(8,128)}, u32[]{:S(2)}) copy-start(f32[2,2,1,1024,512]{4,3,2,1,0:T(8,128)} %param.4) | copy-start | bytes 25165828
  5.2 55.1 %copy-start.2 = (f32[2,1024,1024]{2,1,0:T(8,128)S(1)}, f32[2,1024,1024]{2,1,0:T(8,128)}, u32[]{:S(2)}) copy-start(f32[2,1024,1024]{2,1,0:T(8,128)} %param.5) | copy-start | bytes 25165828
  54.6 5.7 %copy-start = (f32[2,2,1024,1024]{3,2,1,0:T(8,128)}, f32[2,2,1024,1024]{3,2,1,0:T(8,128)S(1)}, u32[]{:S(2)}) copy-start(f32[2,2,1024,1024]{3,2,1,0:T(8,128)S(1)} %get-tuple-element.7) | copy-start | bytes 50331652
  69.0 61.3 %slice-start = ((s8[16777216]{0:T(1024)(128)(4,1)}), s8[4194304]{0:T(1024)(128)(4,1)S(1)}, s32[]{:S(2)}) async-start(s8[16777216]{0:T(1024)(128)(4,1)} %bitcast.48), calls=%async_computation | async-start | bytes 8388608
  69.0 61.3 %slice-start.1 = ((s8[16777216]{0:T(1024)(128)(4,1)}), s8[4194304]{0:T(1024)(128)(4,1)S(1)}, s32[]{:S(2)}) async-start(s8[16777216]{0:T(1024)(128)(4,1)} %bitcast.48), calls=%async_computation.1 | async-start | bytes 8388608
  69.0 61.3 %slice-start.2 = ((s8[16777216]{0:T(1024)(128)(4,1)}), s8[4194304]{0:T(1024)(128)(4,1)S(1)}, s32[]{:S(2)}) async-start(s8[16777216]{0:T(1024)(128)(4,1)} %bitcast.48), calls=%async_computation.2 | async-start | bytes 8388608
  79.4 51.0 %slice-start.3 = ((s8[16777216]{0:T(1024)(128)(4,1)}), s8[4194304]{0:T(1024)(128)(4,1)S(1)}, s32[]{:S(2)}) async-start(s8[16777216]{0:T(1024)(128)(4,1)} %bitcast.48), calls=%async_computation.3 | async-start | bytes 8388608

commit v2 on v1

--- a/solution.py
+++ b/solution.py
@@ -11,6 +11,7 @@
 MESH = pl.DeviceIdType.MESH
 TREES = 3
 CHUNK = 32
+SLACK = 4
 
 
 def grid_of(n):
@@ -158,7 +159,7 @@
 
     def step(s, carry):
         for t in range(TREES):
-            j = s - level[t]
+            j = s - SLACK * level[t]
 
             @pl.when((j >= 0) & (j < counts[t]))
             def _():
@@ -175,7 +176,7 @@
         return carry
 
     deepest = max(max(v) for v in levels)
-    lax.fori_loop(0, max(counts) + deepest, step, 0)
+    lax.fori_loop(0, max(counts) + SLACK * deepest, step, 0)
 
     for t in range(TREES):
 

time: 139 us -> 108 us (0.78)
  Pallas kernels: 94.7 us -> 63.6 us
    pallas_call x2, Pallas kernels: 94.7 us -> 63.6 us  [spread(): pl.pallas_call(functools.partial(spread_kernel, n, root, exchange), out_s...]
where the time goes in v2:
time: 108 us
  Pallas kernels  63.6 us (59%)
  matrix products  31.3 us (29%)
  local copies, waits for them, and re-layouts  12.7 us (12%)
    pallas_call x2, Pallas kernels, spread(): pl.pallas_call(functools.partial(spread_kernel, n, root, exchange), out_s...  63.6 us
    dot_general x1, matrix products, per_device(): sectioned = own - dot(tall[0], solved0).reshape(slots, rows, width)  10.4 us
    unnamed x14, local copies, waits for them, and re-layouts  9.13 us
    dot_general x1, matrix products, per_device(): updated = sectioned - dot(tall[1], solved1).reshape(slots, rows, width)  8.46 us
    dot_general x1, matrix products, per_device(): solved0 = dot(inverses[0], first)  6.86 us
    dot_general x1, matrix products, per_device(): solved1 = spread(dot(inverses[1], sectioned[0]), n, 1)  5.63 us

profile of v2, /device:TPU:24, one launch (start us, length us, event | category | flops | bytes accessed | tf_op | source)
XLA Modules:
  0.0 107.8 jit_solution(5763651615848628939)
XLA Ops:
  0.0 1.8 %slice_bitcast_fusion.2.refs_0_ = f32[1024,512]{1,0:T(8,128)S(1)} fusion(f32[2,1,1024,512]{3,2,1,0:T(8,128)} %param.3), kind=kLoop, calls=%fused_computation.18 | loop fusion | bytes 4194304 | tf_op jit(solution)/shard_map/squeeze | solution.py:239
  1.8 0.0 copy-start.1
  1.8 3.4 %copy-done.1 = f32[2,2,1,1024,512]{4,3,2,1,0:T(8,128)S(1)} copy-done((f32[2,2,1,1024,512]{4,3,2,1,0:T(8,128)S(1)}, f32[2,2,1,1024,512]{4,3,2,1,0:T(8,128)}, u32[]{:S(2)}) %copy-start.1) | copy-done | bytes 8388632
  5.2 0.0 copy-start.2
  5.2 33.6 %shard_map.37 = (f32[1024,512]{1,0:T(8,128)S(1)}, f32[2,2,1024,1024]{3,2,1,0:T(8,128)S(1)}) custom-call(f32[1024,512]{1,0:T(8,128)S(1)} %slice_bitcast_fusion.2.refs_0_, f32[2,2,1024,512]{3,2,1,0:T(8,128)S(1)} %bitcast.50), custom_call_target="tpu_custom_call" | custom-call | tf_op jit(solution)/shard_map/pallas_call | solution.py:217
  38.8 0.0 copy-start
  38.8 5.7 %copy-done = f32[2,2,1024,1024]{3,2,1,0:T(8,128)} copy-done((f32[2,2,1024,1024]{3,2,1,0:T(8,128)}, f32[2,2,1024,1024]{3,2,1,0:T(8,128)S(1)}, u32[]{:S(2)}) %copy-start) | copy-done | bytes 16777240
  44.5 0.0 copy-done.2
  44.5 6.9 %fusion.8 = f32[512,1024]{1,0:T(8,128)S(1)} fusion(f32[1024,512]{1,0:T(8,128)S(1)} %get-tuple-element.8, f32[2,1024,1024]{2,1,0:T(8,128)S(1)} %copy-done.2), kind=kOutput, calls=%fused_computation.8 | convolution fusion | flops 3221225472 | bytes 8388608 | tf_op jit(solution)/shard_map/dot_general | solution.py:240
  51.4 1.8 %copy.4 = f32[1024,512]{1,0:T(8,128)} copy(f32[1024,512]{0,1:T(8,128)S(1)} %bitcast.51) | data formatting | bytes 4194304 | tf_op jit(solution)/shard_map/dot_general | solution.py:240
  53.2 0.0 slice-start
  53.2 0.0 slice-start.1
  53.2 0.0 slice-start.2
  53.2 10.4 %fusion.10 = f32[2,1024,512]{2,1,0:T(8,128)S(1)} fusion(f32[2,1,1024,512]{3,2,1,0:T(8,128)} %param.3, f32[1024,512]{1,0:T(8,128)} %copy.4, pred[2]{0:T(512)(128)(4,1)S(1)} %get-tuple-element.10, f32[512,1024]{1,0:T(8,128)S(1)} %fusion.8, f32[2,2,1024,1024]{3,2,1,0:T(8,128)} %copy-done), kind=kOutput, calls=%fused_computation.11 | convolution fusion | flops 6444548096 | bytes 20971522 | tf_op jit(solution)/shard_map/dot_general | solution.py:242
  63.6 0.0 slice-start.3
  63.6 5.6 %fusion.19.refs_0_ = f32[1024,512]{1,0:T(8,128)S(1)} fusion(f32[2,1024,1024]{2,1,0:T(8,128)} %param.5, f32[2,1024,512]{2,1,0:T(8,128)S(1)} %fusion.10), kind=kOutput, calls=%fused_computation.19 | convolution fusion | flops 3221225472 | bytes 8388608 | tf_op jit(solution)/shard_map/dot_general | solution.py:244
  69.2 30.0 %shard_map.38 = f32[1024,512]{1,0:T(8,128)S(1)} custom-call(f32[1024,512]{1,0:T(8,128)S(1)} %fusion.19.refs_0_), custom_call_target="tpu_custom_call" | custom-call | tf_op jit(solution)/shard_map/pallas_call | solution.py:217
  99.3 0.0 slice-done
  99.3 0.0 slice-done.1
  99.3 0.0 slice-done.2
  99.3 0.0 slice-done.3
  99.3 8.5 %select_bitcast_fusion = f32[2,1,1024,512]{3,2,1,0:T(8,128)} fusion(f32[2,1024,512]{2,1,0:T(8,128)S(1)} %fusion.10, f32[1024,512]{1,0:T(8,128)S(1)} %shard_map.38, pred[2]{0:T(512)(128)(4,1)S(1)} %get-tuple-element.9, pred[2]{0:T(512)(128)(4,1)S(1)} %broadcast_compare_fusion.2, f32[2,2,1024,1024]{3,2,1,0:T(8,128)S(1)} %bitcast.49), kind=kOutput, calls=%fused_computation.12 | convolution fusion | flops 6445596672 | bytes 20972544 | tf_op jit(solution)/shard_map/dot_general | solution.py:245
  (3 shorter events, 0.0 us)
Async XLA Ops:
  1.8 3.4 %copy-start.1 = (f32[2,2,1,1024,512]{4,3,2,1,0:T(8,128)S(1)}, f32[2,2,1,1024,512]{4,3,2,1,0:T(8,128)}, u32[]{:S(2)}) copy-start(f32[2,2,1,1024,512]{4,3,2,1,0:T(8,128)} %param.4) | copy-start | bytes 25165828
  5.2 39.3 %copy-start.2 = (f32[2,1024,1024]{2,1,0:T(8,128)S(1)}, f32[2,1024,1024]{2,1,0:T(8,128)}, u32[]{:S(2)}) copy-start(f32[2,1024,1024]{2,1,0:T(8,128)} %param.5) | copy-start | bytes 25165828
  38.8 5.7 %copy-start = (f32[2,2,1024,1024]{3,2,1,0:T(8,128)}, f32[2,2,1024,1024]{3,2,1,0:T(8,128)S(1)}, u32[]{:S(2)}) copy-start(f32[2,2,1024,1024]{3,2,1,0:T(8,128)S(1)} %get-tuple-element.7) | copy-start | bytes 50331652
  53.2 46.1 %slice-start = ((s8[16777216]{0:T(1024)(128)(4,1)}), s8[4194304]{0:T(1024)(128)(4,1)S(1)}, s32[]{:S(2)}) async-start(s8[16777216]{0:T(1024)(128)(4,1)} %bitcast.48), calls=%async_computation | async-start | bytes 8388608
  53.2 46.1 %slice-start.1 = ((s8[16777216]{0:T(1024)(128)(4,1)}), s8[4194304]{0:T(1024)(128)(4,1)S(1)}, s32[]{:S(2)}) async-start(s8[16777216]{0:T(1024)(128)(4,1)} %bitcast.48), calls=%async_computation.1 | async-start | bytes 8388608
  53.2 46.1 %slice-start.2 = ((s8[16777216]{0:T(1024)(128)(4,1)}), s8[4194304]{0:T(1024)(128)(4,1)S(1)}, s32[]{:S(2)}) async-start(s8[16777216]{0:T(1024)(128)(4,1)} %bitcast.48), calls=%async_computation.2 | async-start | bytes 8388608
  63.6 35.7 %slice-start.3 = ((s8[16777216]{0:T(1024)(128)(4,1)}), s8[4194304]{0:T(1024)(128)(4,1)S(1)}, s32[]{:S(2)}) async-start(s8[16777216]{0:T(1024)(128)(4,1)} %bitcast.48), calls=%async_computation.3 | async-start | bytes 8388608
